TPU v7x, 32 devices: a whole 2x2x4 slice. The times are simulated.
32 devices in a mesh: act: 8 (over y, x, core), pix: 4 (over z).
Axes of the slice: x: 2, y: 2, z: 4, core: 2. Of those that a mesh axis runs over, the one named last changes fastest.
Arguments:
- pixel_index: int32 [4, 512], P('pix'), may hold values from 0 to 65535
- act_map: int32 [32768], P('act'), may hold values from 0 to 32767, each once
- omega: bfloat16 [32768, 128], P('act'), may hold values from -6 to 6
- pupil_field: float32 [4, 2, 32768], P('pix', None, 'act'), may hold values from -6 to 6
- channel_scale: float32 [4], P('pix'), may hold values from 0.9 to 1.1
- channel_flux: float32 [4], P('pix'), may hold values from 0.3 to 3
Outputs:
- basis_out: float32 [4, 1024, 128], P('pix', 'act')
- projection: float32 [128, 32768], P('pix', 'act')
- r_factor: float32 [128, 128], replicated
Inputs may be any that keep to these rules, and one draw needn't show every extreme that they name: `act_map`: every number of 0 to 32767 appears once. `pixel_index`: pixels of a channel may repeat.
All inputs are finite; a program needn't handle non-finite values.
Results may differ from a plain program's by a relative error of at most 0.0048.
Values may be sent and summed in bfloat16 or wider, within the bound.
A program may use at most 64 MiB of HBM per device.

v0:
```python
import math

import jax
import jax.numpy as jnp
from jax import lax
from jax.sharding import PartitionSpec as P

GRID = 128
FOCAL = 256
RANK = 128
ACT = 32768


TWO_PI = 2.0 * math.pi
INFL_RATE = 4.5
DEFOCUS_RATE = 6.0


def jacobian_rows(pixels, wave_scale, flux_level, codes, field_re, field_im):
    delta_u = pixels // FOCAL - FOCAL // 2
    delta_v = pixels % FOCAL - FOCAL // 2
    mirror = codes // (GRID * GRID)
    column_x = codes // GRID % GRID - GRID // 2
    column_y = codes % GRID - GRID // 2
    phase_int = delta_u[:, None] * column_x[None, :] + delta_v[:, None] * column_y[None, :]
    radius = (delta_u * delta_u + delta_v * delta_v).astype(jnp.float32)
    amplitude = flux_level * jnp.exp(-INFL_RATE * radius / (FOCAL * FOCAL))
    defocus = radius * (TWO_PI * DEFOCUS_RATE / (FOCAL * FOCAL)) / wave_scale
    phase_angle = mirror.astype(jnp.float32)[None, :] * defocus[
        :, None
    ] - TWO_PI / FOCAL * wave_scale * phase_int.astype(jnp.float32)
    cosine = jnp.cos(phase_angle)
    sine_part = jnp.sin(phase_angle)
    real_part = amplitude[:, None] * (field_re[None, :] * cosine - field_im[None, :] * sine_part)
    imag_part = amplitude[:, None] * (field_re[None, :] * sine_part + field_im[None, :] * cosine)
    stacked = jnp.stack([real_part, imag_part], axis=1)
    return stacked.reshape(2 * pixels.shape[0], codes.shape[0]).astype(jnp.bfloat16)


def gram_of(sketch):
    return lax.dot_general(
        sketch,
        sketch,
        (((0,), (0,)), ((), ())),
        precision=lax.Precision.HIGHEST,
        preferred_element_type=jnp.float32,
    )


def orthonormal(sketch, gram_matrix):
    lower_factor = jnp.linalg.cholesky(gram_matrix)
    basis = jax.scipy.linalg.solve_triangular(lower_factor, sketch.T, lower=True).T
    return (lower_factor, basis)


def on_device(pixel_index, act_map, omega, pupil_field, channel_scale, channel_flux):
    pixels = pixel_index[0]
    rows_dev = 2 * pixels.shape[0]
    act_cols = act_map.shape[0]
    act_count = lax.axis_size("act")
    pix_count = lax.axis_size("pix")
    total_rows = rows_dev * pix_count
    share_rows = rows_dev // act_count
    wave_scale = channel_scale[0]
    flux_level = channel_flux[0]
    field_re = pupil_field[0, 0]
    field_im = pupil_field[0, 1]
    padded = jnp.concatenate([pixels, pixels[:1]])
    rows_all = jacobian_rows(padded, wave_scale, flux_level, act_map, field_re, field_im)
    stored = lax.dynamic_slice_in_dim(rows_all, 0 % 2, rows_dev, 0)

    def rows_of():
        return stored

    sketch = lax.psum(jnp.dot(rows_of(), omega, preferred_element_type=jnp.float32), "act")
    gram_matrix = lax.psum(gram_of(sketch), "pix")
    lower_factor, basis = orthonormal(sketch, gram_matrix)
    own_basis = lax.dynamic_slice_in_dim(basis, lax.axis_index("act") * share_rows, share_rows, 0)
    coarse = basis.astype(jnp.bfloat16)
    block_rows = math.gcd(rows_dev, 2048)

    def add_block(block_id, total_sum):
        jacobian = rows_of()
        return total_sum + lax.dot_general(
            coarse, jacobian, (((0,), (0,)), ((), ())), preferred_element_type=jnp.float32
        )

    partial_value = lax.fori_loop(
        0, rows_dev // block_rows, add_block, jnp.zeros((RANK, act_cols), jnp.float32)
    )
    projection = lax.psum_scatter(partial_value, "pix", scatter_dimension=0, tiled=True)
    basis_out = (own_basis * math.sqrt(total_rows)).reshape(1, share_rows, RANK)
    r_factor = lower_factor.T / math.sqrt(total_rows * ACT)
    return (basis_out, projection, r_factor)


def solution(mesh):
    return jax.shard_map(
        on_device,
        mesh=mesh,
        in_specs=(
            P("pix", None),
            P("act"),
            P("act", None),
            P("pix", None, "act"),
            P("pix"),
            P("pix"),
        ),
        out_specs=(P("pix", "act", None), P("pix", "act"), P()),
        check_vma=False,
    )
```

profile of v0, /device:TPU:0, one launch (start us, length us, event | category | flops | bytes accessed | tf_op | source)
XLA Modules:
  0.0 269.5 jit_solution(8104190666320655889)
XLA Ops:
  7.2 0.0 copy-start
  7.2 0.0 all-reduce.3.cloned.1.call-start
  7.2 1.2 slice.23
  9.1 1.3 fusion.15
  10.5 1.4 exponential_multiply_fusion
  12.5 0.8 fusion.8
  13.2 0.9 fusion.21
  14.1 1.3 multiply_divide_fusion
  15.5 35.5 %multiply_convert_fusion.1 = (bf16[513,1,4096]{2,0,1:T(8,128)(2,1)S(1)}, bf16[513,1,4096]{2,0,1:T(8,128)(2,1)}) fusion(f32[4096]{0:T(1024)S(1)} %bitcast.29, s32[4096]{0:T(1024)S(1)} %get-tuple-element.33, s32[513]{0:T(1024)S(1)} %fusion.15, s32[4096]{0:T(1024)S(1)} %get-tuple-element.34, s32[513]{0:T(1024)S(1)} %get-tuple-element.25, f32[]{:T(128)S(6)} %mul_shard_map.3, ...), kind=kLoop, calls=%fused_computation.1 | loop fusion | flops 35721216 | bytes 8495124 | tf_op jit(solution)/shard_map/convert
  51.0 6.2 %pad_maximum_fusion = bf16[512,2,4096]{2,0,1:T(8,128)(2,1)} fusion(bf16[513,1,4096]{2,0,1:T(8,128)(2,1)} %get-tuple-element.27, bf16[513,1,4096]{2,0,1:T(8,128)(2,1)S(1)} %get-tuple-element.26), kind=kLoop, calls=%fused_computation.5 | loop fusion | flops 16777216 | bytes 16793600 | tf_op jit(solution)/shard_map/stack | solution.py:36
  57.2 16.4 %copy.15 = bf16[512,2,4096]{2,1,0:T(2,128)(2,1)} copy(bf16[512,2,4096]{2,0,1:T(8,128)(2,1)} %pad_maximum_fusion) | data formatting | bytes 16777216 | tf_op jit(solution)/shard_map/dynamic_slice | solution.py:70
  73.6 13.1 %dynamic_slice.9 = bf16[1024,4096]{1,0:T(8,128)(2,1)} reshape(bf16[512,2,4096]{2,1,0:T(2,128)(2,1)} %copy.15) | data formatting | bytes 16777216 | tf_op jit(solution)/shard_map/dynamic_slice | solution.py:70
  86.7 0.0 copy-done
  86.7 6.5 %fusion.22 = f32[1024,128]{1,0:T(8,128)} fusion(bf16[1024,4096]{1,0:T(8,128)(2,1)} %dynamic_slice.9, bf16[4096,128]{1,0:T(8,128)(2,1)S(1)} %copy-done), kind=kOutput, calls=%fused_computation.56 | convolution fusion | flops 1073741824 | bytes 9961472 | tf_op jit(solution)/shard_map/dot_general | solution.py:75
  93.2 0.0 all-reduce.3.cloned.1.call-update
  93.2 0.2 all-reduce.5.cloned.1.call-start
  93.4 57.2 %all-reduce.3.cloned.1.call-done = f32[1024,128]{1,0:T(8,128)} async-done(((f32[1024,128]{1,0:T(8,128)}), f32[1024,128]{1,0:T(8,128)}) %all-reduce.3.cloned.1.call-update) | async-done | bytes 524304 | tf_op jit(solution)/shard_map/psum | solution.py:75
  150.6 2.8 %fusion.23 = f32[128,128]{0,1:T(8,128)} fusion(f32[1024,128]{1,0:T(8,128)} %all-reduce.3.cloned.1.call-done), kind=kOutput, calls=%fused_computation.57 | convolution fusion | flops 201326592 | bytes 589824 | tf_op jit(solution)/shard_map/dot_general | solution.py:41
  153.4 0.0 all-reduce.5.cloned.1.call-update
  153.5 0.0 reduce-scatter.2.cloned.1.call-start
  153.5 33.4 %all-reduce.5.cloned.1.call-done = f32[128,128]{0,1:T(8,128)} async-done(((f32[128,128]{0,1:T(8,128)}), f32[128,128]{0,1:T(8,128)}) %all-reduce.5.cloned.1.call-update) | async-done | bytes 65552 | tf_op jit(solution)/shard_map/psum | solution.py:76
  186.9 0.9 copy.17
  187.9 0.9 fusion.6
  188.7 11.7 %cholesky.16 = f32[128,128]{1,0:T(8,128)S(1)} custom-call(f32[128,128]{1,0:T(8,128)S(1)} %fusion.6), custom_call_target="Cholesky" | custom-call | tf_op jit(solution)/shard_map/jit(cholesky)/cholesky | solution.py:51
  200.5 0.6 compare_reduce_fusion
  201.1 0.7 multiply_bitcast_fusion
  201.8 9.8 %custom-call.7 = f32[1,128,128]{1,2,0:T(8,128)S(1)} custom-call(f32[1,128,128]{2,1,0:T(8,128)S(1)} %get-tuple-element.29), custom_call_target="InvertDiagBlocksLowerTriangular" | custom-call | tf_op jit(solution)/shard_map/jit(_solve_triangular)/triangular_solve | solution.py:52
  211.6 1.6 fusion.4
  213.2 6.1 %fusion.2 = f32[128,4096]{1,0:T(8,128)} fusion(bf16[1024,4096]{1,0:T(8,128)(2,1)} %dynamic_slice.9, f32[1024,128]{1,0:T(8,128)S(1)} %fusion.4), kind=kOutput, calls=%fused_computation.6 | convolution fusion | flops 1073872896 | bytes 11010048 | tf_op jit(solution)/shard_map/while/body/eval_jaxpr/dot_general | solution.py:84
  219.3 0.0 reduce-scatter.2.cloned.1.call-update
  219.3 0.7 copy.18
  220.0 0.6 multiply_bitcast_fusion.1
  220.7 42.4 %reduce-scatter.2.cloned.1.call-done = f32[32,4096]{1,0:T(8,128)} async-done(((f32[128,4096]{1,0:T(8,128)}), f32[32,4096]{1,0:T(8,128)}) %reduce-scatter.2.cloned.1.call-update) | async-done | bytes 524304 | tf_op jit(solution)/shard_map/reduce_scatter | solution.py:91
  (1 shorter events, 0.0 us)
Async XLA Ops:
  7.2 79.5 %copy-start = (bf16[4096,128]{1,0:T(8,128)(2,1)S(1)}, bf16[4096,128]{1,0:T(8,128)(2,1)}, u32[]{:S(2)}) copy-start(bf16[4096,128]{1,0:T(8,128)(2,1)} %param.8) | copy-start | bytes 3145732
  7.2 143.4 %all-reduce.3.cloned.1.call-start = ((), (), s32[]{:S(2)}) async-start(), calls=%async_computation.1 | async-start | bytes 1048576 | tf_op jit(solution)/shard_map/psum | solution.py:75
  93.2 93.7 %all-reduce.5.cloned.1.call-start = ((), (), s32[]{:S(2)}) async-start(), calls=%async_computation.2 | async-start | bytes 131072 | tf_op jit(solution)/shard_map/psum | solution.py:76
  153.5 109.6 %reduce-scatter.2.cloned.1.call-start = ((), (), s32[]{:S(2)}) async-start(), calls=%async_computation.3 | async-start | bytes 2621440 | tf_op jit(solution)/shard_map/reduce_scatter | solution.py:91
Sparse Core Ops, SparseCore 0:
  93.3 57.2 all-reduce.2
  153.6 33.2 all-reduce.4
  219.4 43.5 reduce-scatter.1
where the time goes:
time: 271 us; the launch traced here: 270 us
  waiting for transfers between devices  133 us (49%)
  other arithmetic  70.9 us (26%)
  local copies, waits for them, and re-layouts  33.3 us (12%)
  matrix products  17 us (6%)
  between operations  15.1 us (6%)
    psum x1, waiting for transfers between devices, on_device(): lax.psum(jnp.dot(rows_of(), omega, preferred_element_type=jnp.float32), '...  57.2 us
    reduce_scatter x1, waiting for transfers between devices, on_device(): lax.psum_scatter(partial_value, 'pix', scatter_dimension=0, tiled=True)  42.4 us
    another operation x1, other arithmetic  35.5 us
    psum x1, waiting for transfers between devices, on_device(): gram_matrix = lax.psum(gram_of(sketch), 'pix')  33.4 us
    dynamic_slice x2, local copies, waits for them, and re-layouts, on_device(): stored = lax.dynamic_slice_in_dim(rows_all, 0 % 2, rows_dev, 0)  29.5 us
    another operation x3, other arithmetic, orthonormal(): lower_factor = jnp.linalg.cholesky(gram_matrix)  12.4 us
    another operation x1, other arithmetic, orthonormal(): jax.scipy.linalg.solve_triangular(lower_factor, sketch.T, lower=True)  9.81 us
    dot_general x1, matrix products, on_device(): jnp.dot(rows_of(), omega, preferred_element_type=jnp.float32)  6.5 us
  transfers between devices with their start and end apart: 3, of which 3 were waited for; matrix products, arithmetic and copies ran while one was open for 1% of the time, Pallas kernels for 0%

commit v1 on v0

v1 whole, which is shorter than its diff:
```python
import functools
import math

import jax
import jax.numpy as jnp
from jax import lax
from jax.experimental import pallas as pl
from jax.experimental.pallas import tpu as pltpu
from jax.sharding import PartitionSpec as P

GRID = 128
FOCAL = 256
RANK = 128
ACT = 32768
PANEL = 8
COLS = 1024

INFL_RATE = 4.5
DEFOCUS_RATE = 6.0
MESH = pl.DeviceIdType.MESH
HIGH = lax.Precision.HIGHEST

SIN_POLY = (4.4428679, -7.30744342, 3.59478808, -0.78437403)
COS_POLY = (1.4142135, -6.97885099, 5.73946117, -1.88356299, 0.310698192)


def split3(value):
    high = lax.reduce_precision(value, 8, 7)
    middle = lax.reduce_precision(value - high, 8, 7)
    low = lax.reduce_precision(value - high - middle, 8, 7)
    return [high, middle, low]


def pixel_features(pixels, wave_scale, flux_level):
    u = (pixels // FOCAL - FOCAL // 2).astype(jnp.float32)
    v = (pixels % FOCAL - FOCAL // 2).astype(jnp.float32)
    radius = u * u + v * v
    amplitude = flux_level * jnp.exp(-INFL_RATE * radius / (FOCAL * FOCAL))
    step_u = -(wave_scale / FOCAL) * u
    step_v = -(wave_scale / FOCAL) * v
    defocus = radius * (DEFOCUS_RATE / (FOCAL * FOCAL)) / wave_scale
    rows = []
    for turns in (step_u, step_v, defocus):
        rows += split3(turns - jnp.round(turns))
    one, zero = jnp.ones_like(u), jnp.zeros_like(u)
    rows += [one] * 3 + [zero] * 4
    high, middle, low = split3(amplitude)
    rows += [high, high, high, middle, middle, low] + [zero] * 10
    return jnp.stack(rows)


def actuator_features(codes, field):
    mirror = (codes // (GRID * GRID)).astype(jnp.float32)
    x = (codes // GRID % GRID - GRID // 2).astype(jnp.float32)
    y = (codes % GRID - GRID // 2).astype(jnp.float32)
    zero = jnp.zeros_like(x)
    angle = jnp.arctan2(field[1], field[0]) * (0.5 / math.pi)
    magnitude = jnp.sqrt(field[0] * field[0] + field[1] * field[1])
    rows = [x] * 3 + [y] * 3 + [mirror] * 3 + split3(angle) + [zero] * 4
    high, middle, low = split3(magnitude)
    rows += [high, middle, low, high, middle, high] + [zero] * 10
    return jnp.stack(rows).astype(jnp.bfloat16)


def dot_first(lhs, rhs, precision=None):
    return lax.dot_general(
        lhs, rhs, (((0,), (0,)), ((), ())), precision=precision, preferred_element_type=jnp.float32
    )


def jacobian_tile(pix, act):
    turns = dot_first(pix[:16], act[:16])
    scale = dot_first(pix[16:], act[16:])
    f = turns - jnp.round(turns)
    q = f * f
    sine = SIN_POLY[-1]
    for coefficient in SIN_POLY[-2::-1]:
        sine = sine * q + coefficient
    sine = sine * f
    cosine = COS_POLY[-1]
    for coefficient in COS_POLY[-2::-1]:
        cosine = cosine * q + coefficient
    real = (scale * (1.0 - sine * sine)).astype(jnp.bfloat16)
    imag = (scale * (sine * cosine)).astype(jnp.bfloat16)
    return jnp.concatenate([real, imag], axis=0)


def kernel(
    A, Z, pix_ref, act_ref, omega_ref, basis_ref, proj_ref, rfac_ref,
    pix_all, act_all, rs_send, rs_recv, own, sk_all, jac, aug, tmat, ex_send, ex_recv,
    feat_s, feat_r, rs_s, rs_r, z_s, z_r, pl_s, pl_r, ex_s, ex_r, local_s,
):
    ai, zi = lax.axis_index("act"), lax.axis_index("pix")
    rows_blk = rs_send.shape[1]
    cols = act_ref.shape[1]
    part = act_all.shape[2]
    share = RANK // Z
    chunk = min(COLS, cols)

    def act_peer(k):
        return lax.rem(ai + k, A)

    def pix_peer(k):
        return lax.rem(zi + k, Z)

    barrier = pltpu.get_barrier_semaphore()

    @pl.loop(1, A)
    def _(k):
        pl.semaphore_signal(barrier, inc=1, device_id=(act_peer(k), zi), device_id_type=MESH)

    for k in range(1, Z):
        pl.semaphore_signal(barrier, inc=1, device_id=(ai, pix_peer(k)), device_id_type=MESH)
    pl.semaphore_wait(barrier, A - 1 + Z - 1)

    def feat_copies(peer, slot):
        return (
            pltpu.make_async_remote_copy(
                src_ref=pix_ref, dst_ref=pix_all.at[slot], send_sem=feat_s.at[peer, 0],
                recv_sem=feat_r.at[slot, 0], device_id=(ai, peer), device_id_type=MESH),
            pltpu.make_async_remote_copy(
                src_ref=act_ref.at[:, pl.ds(pl.multiple_of(peer * part, part), part)],
                dst_ref=act_all.at[slot], send_sem=feat_s.at[peer, 1],
                recv_sem=feat_r.at[slot, 1], device_id=(ai, peer), device_id_type=MESH),
        )

    for k in range(1, Z):
        for copy in feat_copies(pix_peer(k), zi):
            copy.start()
    mine = pl.ds(pl.multiple_of(zi * part, part), part)
    act_all[zi] = act_ref[:, mine]
    pix_all[zi] = pix_ref[...]

    def rs_copy(peer, slot):
        return pltpu.make_async_remote_copy(
            src_ref=rs_send.at[peer], dst_ref=rs_recv.at[slot], send_sem=rs_s.at[peer],
            recv_sem=rs_r.at[slot], device_id=(peer, zi), device_id_type=MESH)

    def partial(block):
        total = jnp.zeros((rows_blk, RANK), jnp.float32)
        for start in range(0, cols, chunk):
            tile = jacobian_tile(pix_ref[block], act_ref[:, start:start + chunk])
            total += jnp.dot(
                tile, omega_ref[start:start + chunk], preferred_element_type=jnp.float32)
        rs_send[block] = total

    @pl.loop(1, A)
    def _(k):
        block = act_peer(k)
        partial(block)
        rs_copy(block, ai).start()

    partial(ai)
    own[...] = rs_send[ai]

    @pl.loop(1, A)
    def _(k):
        peer = act_peer(A - k)
        rs_copy(peer, peer).wait_recv()
        own[...] += rs_recv[peer]

    def block_of(channel, shard):
        return pl.ds(pl.multiple_of((channel * A + shard) * rows_blk, rows_blk), rows_blk)

    def z_copy(peer, slot):
        return pltpu.make_async_remote_copy(
            src_ref=sk_all.at[block_of(slot, ai)], dst_ref=sk_all.at[block_of(slot, ai)],
            send_sem=z_s.at[peer], recv_sem=z_r.at[slot], device_id=(ai, peer), device_id_type=MESH)

    def plane_copy(channel, peer, slot):
        return pltpu.make_async_remote_copy(
            src_ref=sk_all.at[block_of(channel, slot)], dst_ref=sk_all.at[block_of(channel, slot)],
            send_sem=pl_s.at[channel, peer], recv_sem=pl_r.at[channel, slot],
            device_id=(peer, zi), device_id_type=MESH)

    sk_all[block_of(zi, ai)] = own[...].astype(jnp.bfloat16)
    for k in range(1, Z):
        z_copy(pix_peer(k), zi).start()

    def spread(channel):
        @pl.loop(1, A)
        def _(k):
            plane_copy(channel, act_peer(k), ai).start()

    def fill(channel):
        @pl.loop(0, A)
        def _(a):
            jac[block_of(channel, a)] = jacobian_tile(pix_all[channel, a], act_all[channel])

    spread(zi)
    fill(zi)
    for k in range(1, Z):
        z_copy(pix_peer(k), pix_peer(k)).wait_recv()
        spread(pix_peer(k))
    for k in range(1, Z):
        for copy in feat_copies(pix_peer(k), pix_peer(k)):
            copy.wait_recv()
    @pl.loop(1, Z)
    def _(k):
        fill(pix_peer(k))

    @pl.loop(0, Z)
    def _(c):
        @pl.loop(1, A)
        def _(k):
            plane_copy(c, act_peer(k), act_peer(k)).wait_recv()

    sketch = sk_all[...]
    aug[:, :RANK] = dot_first(sketch, sketch)
    row_id = lax.broadcasted_iota(jnp.int32, (RANK, RANK), 0)
    col_id = lax.broadcasted_iota(jnp.int32, (RANK, RANK), 1)
    aug[:, RANK:] = (row_id == col_id).astype(jnp.float32)
    tmat[...] = jnp.zeros_like(tmat)
    panels = RANK // PANEL
    span = sk_all.shape[0] // panels
    sub = lax.broadcasted_iota(jnp.int32, (PANEL, RANK), 0)
    lane = lax.broadcasted_iota(jnp.int32, (PANEL, RANK), 1)

    @pl.loop(0, panels)
    def _(i):
        at = pl.multiple_of(i * PANEL, PANEL)
        left = aug[pl.ds(at, PANEL), :RANK]
        right = aug[pl.ds(at, PANEL), RANK:]
        rolled = pltpu.roll(left, lax.rem(RANK - at, RANK), 1)
        column = [jnp.broadcast_to(rolled[:, k:k + 1], (PANEL, RANK)) for k in range(PANEL)]
        for k in range(PANEL):
            inverse = lax.rsqrt(column[k][k:k + 1])
            weight = jnp.where(sub > k, column[k] * inverse, 0.0)
            left_row, right_row = left[k:k + 1] * inverse, right[k:k + 1] * inverse
            left = jnp.where(sub == k, left_row, left - weight * left_row)
            right = jnp.where(sub == k, right_row, right - weight * right_row)
            for l in range(k + 1, PANEL):
                column[l] = column[l] - weight * (column[l][k:k + 1] * inverse)
        aug[pl.ds(at, PANEL), :RANK] = left
        aug[pl.ds(at, PANEL), RANK:] = right
        factor = jnp.where(lane >= at + PANEL, left, 0.0)
        both = jnp.concatenate([left, right], axis=1)
        aug[...] = aug[...] - dot_first(factor, both, HIGH)
        rows = pl.ds(pl.multiple_of(i * span, span), span)
        tmat[...] += dot_first(sk_all[rows], jac[rows])

    inverse_l = aug[:, RANK:]
    rfac_ref[...] = jnp.where(col_id >= row_id, aug[:, :RANK], 0.0) * (
        1.0 / math.sqrt(rows_blk * A * Z * ACT))
    projection = jnp.dot(inverse_l, tmat[...], precision=HIGH, preferred_element_type=jnp.float32)
    for z in range(Z):
        ex_send[z] = projection[z * share:(z + 1) * share].astype(jnp.bfloat16)

    def ex_copy(peer, slot):
        return pltpu.make_async_remote_copy(
            src_ref=ex_send.at[peer], dst_ref=ex_recv.at[slot], send_sem=ex_s.at[peer],
            recv_sem=ex_r.at[slot], device_id=(ai, peer), device_id_type=MESH)

    for k in range(1, Z):
        ex_copy(pix_peer(k), zi).start()
    basis = lax.dot_general(
        own[...], inverse_l, (((1,), (1,)), ((), ())), precision=HIGH,
        preferred_element_type=jnp.float32)
    basis_ref[...] = basis * math.sqrt(rows_blk * A * Z)
    proj_ref[:, mine] = ex_send[zi].astype(jnp.float32)

    @pl.loop(1, A)
    def _(k):
        rs_copy(act_peer(k), ai).wait_send()

    for k in range(1, Z):
        for copy in feat_copies(pix_peer(k), zi):
            copy.wait_send()
        z_copy(pix_peer(k), zi).wait_send()

    @pl.loop(0, Z)
    def _(c):
        @pl.loop(1, A)
        def _(k):
            plane_copy(c, act_peer(k), ai).wait_send()

    for k in range(1, Z):
        peer = pix_peer(k)
        ex_copy(peer, peer).wait_recv()
        proj_ref[:, pl.ds(pl.multiple_of(peer * part, part), part)] = ex_recv[peer].astype(
            jnp.float32)
    for k in range(1, Z):
        ex_copy(pix_peer(k), zi).wait_send()


def on_device(pixel_index, act_map, omega, pupil_field, channel_scale, channel_flux):
    A, Z = lax.axis_size("act"), lax.axis_size("pix")
    pixels = pixel_index[0]
    count = pixels.shape[0]
    cols = act_map.shape[0]
    part = cols // Z
    block = count // A
    rows_blk = 2 * block
    pix = pixel_features(pixels, channel_scale[0], channel_flux[0])
    pix = pix.reshape(32, A, block).transpose(1, 0, 2).astype(jnp.bfloat16)
    act = actuator_features(act_map, pupil_field[0])
    vmem = pl.BlockSpec(memory_space=pltpu.VMEM)
    dma = pltpu.SemaphoreType.DMA
    f32, bf16 = jnp.float32, jnp.bfloat16
    basis, projection, r_factor = pl.pallas_call(
        functools.partial(kernel, A, Z),
        out_shape=(
            jax.ShapeDtypeStruct((rows_blk, RANK), f32),
            jax.ShapeDtypeStruct((RANK // Z, cols), f32),
            jax.ShapeDtypeStruct((RANK, RANK), f32),
        ),
        in_specs=[vmem] * 3,
        out_specs=(vmem,) * 3,
        scratch_shapes=[
            pltpu.VMEM((Z, A, 32, block), bf16),
            pltpu.VMEM((Z, 32, part), bf16),
            pltpu.VMEM((A, rows_blk, RANK), f32),
            pltpu.VMEM((A, rows_blk, RANK), f32),
            pltpu.VMEM((rows_blk, RANK), f32),
            pltpu.VMEM((Z * A * rows_blk, RANK), bf16),
            pltpu.VMEM((Z * A * rows_blk, part), bf16),
            pltpu.VMEM((RANK, 2 * RANK), f32),
            pltpu.VMEM((RANK, part), f32),
            pltpu.VMEM((Z, RANK // Z, part), bf16),
            pltpu.VMEM((Z, RANK // Z, part), bf16),
            dma((Z, 2)), dma((Z, 2)), dma((A,)), dma((A,)), dma((Z,)), dma((Z,)),
            dma((Z, A)), dma((Z, A)), dma((Z,)), dma((Z,)), dma,
        ],
        compiler_params=pltpu.CompilerParams(
            collective_id=0, has_side_effects=True, vmem_limit_bytes=48 * 1024 * 1024),
    )(pix, act, omega)
    basis_out = basis.reshape(2, block, RANK).transpose(1, 0, 2).reshape(1, rows_blk, RANK)
    return basis_out, projection, r_factor


def solution(mesh):
    return jax.shard_map(
        on_device,
        mesh=mesh,
        in_specs=(
            P("pix", None),
            P("act"),
            P("act", None),
            P("pix", None, "act"),
            P("pix"),
            P("pix"),
        ),
        out_specs=(P("pix", "act", None), P("pix", "act"), P()),
        check_vma=False,
    )
```

time: 271 us -> 61.3 us (0.23)
  waiting for transfers between devices: 133 us -> 0 us
  other arithmetic: 70.9 us -> 2.76 us
  Pallas kernels: 0 us -> 52.3 us
  local copies, waits for them, and re-layouts: 33.3 us -> 3.87 us
  matrix products: 17 us -> 0 us
  between operations: 15.1 us -> 2.13 us
    psum x2 -> x0, waiting for transfers between devices: 90.6 us -> none  [the longest x1 57.2 us: on_device(): lax.psum(jnp.dot(rows_of(), omega, preferred_element_type=jnp.float32), '...]
    another operation x6 -> x5, other arithmetic: 63.9 us -> 2.05 us
    pallas_call x0 -> x1, Pallas kernels: none -> 52.3 us  [on_device(): pl.pallas_call(functools.partial(kernel, A, Z), out_shape=(jax.ShapeDtype...]
    reduce_scatter x1 -> x0, waiting for transfers between devices: 42.4 us -> none  [on_device(): lax.psum_scatter(partial_value, 'pix', scatter_dimension=0, tiled=True)]
    dynamic_slice x2 -> x0, local copies, waits for them, and re-layouts: 29.5 us -> none  [on_device(): stored = lax.dynamic_slice_in_dim(rows_all, 0 % 2, rows_dev, 0)]
    dot_general x3 -> x0, matrix products: 15.4 us -> none  [the longest x1 6.5 us: on_device(): jnp.dot(rows_of(), omega, preferred_element_type=jnp.float32)]
    div x3 -> x0, other arithmetic: 2.86 us -> none  [the longest x1 1.35 us: jacobian_rows(): defocus = radius * (TWO_PI * DEFOCUS_RATE / (FOCAL * FOCAL)) / wave_scale]
  transfers between devices with their start and end apart: 3 -> 0, of which waited for: 3 -> 0; matrix products, arithmetic and copies ran while one was open for 1% -> 0% of each run, Pallas kernels for 0% -> 0%
where the time goes in v1:
time: 61.3 us; the launch traced here: 61 us
  Pallas kernels  52.3 us (85%)
  local copies, waits for them, and re-layouts  3.87 us (6%)
  other arithmetic  2.76 us (5%)
  between operations  2.13 us (3%)
    pallas_call x1, Pallas kernels, on_device(): pl.pallas_call(functools.partial(kernel, A, Z), out_shape=(jax.ShapeDtype...  52.3 us
    another operation x5, other arithmetic  2.05 us
    unnamed x4, local copies, waits for them, and re-layouts  1.43 us

profile of v1, /device:TPU:0, one launch (start us, length us, event | category | flops | bytes accessed | tf_op | source)
XLA Modules:
  0.0 61.0 jit_solution(12666939044000692189)
XLA Ops:
  0.6 0.0 copy-start
  2.0 0.7 %exponential_multiply_fusion = (f32[1,512]{1,0:T(1,128)S(1)}, f32[1,512]{1,0:T(1,128)S(1)}, f32[1,512]{1,0:T(1,128)S(1)}, s32[1,512]{1,0:T(1,128)S(1)}) fusion(f32[]{:T(128)} %bitcast.23, s32[1,512]{1,0:T(1,128)} %param.6), kind=kLoop, calls=%fused_computation.80 | loop fusion | flops 14336 | bytes 10244 | tf_op jit(solution)/shard_map/mul | solution.py:38
  2.7 0.1 fusion.34
  2.8 0.1 stack.124
  2.9 0.1 reshape.170
  3.0 0.1 reshape.169
  3.0 0.1 stack.121
  3.1 0.1 stack.122
  3.2 0.1 stack.123
  3.3 0.1 fusion.36
  3.3 0.1 stack.120
  3.4 0.1 stack.119
  3.5 0.1 stack.118
  3.6 0.1 stack.115
  3.7 0.1 stack.116
  3.8 0.1 stack.117
  3.9 0.2 stack.107
  4.1 0.8 %fusion.13 = (bf16[4096]{0:T(1024)(128)(2,1)S(1)}, bf16[4096]{0:T(1024)(128)(2,1)S(1)}, bf16[4096]{0:T(1024)(128)(2,1)S(1)}) fusion(s32[4096]{0:T(1024)} %param.7), kind=kLoop, calls=%fused_computation.32 | loop fusion | flops 196608 | bytes 40960 | tf_op jit(solution)/shard_map/convert.6
  4.9 1.1 %fusion.3 = (bf16[1,4096]{1,0:T(2,128)(2,1)S(1)}, f32[1,1,4096]{2,1,0:T(1,128)S(1)}, bf16[1,4096]{1,0:T(2,128)(2,1)S(1)}, f32[1,1,4096]{2,1,0:T(1,128)S(1)}) fusion(f32[1,2,4096]{2,1,0:T(2,128)} %param.9), kind=kLoop, calls=%fused_computation.22 | loop fusion | flops 65536 | bytes 81920 | tf_op jit(solution)/shard_map/convert.15
  6.2 0.5 stack.114.act_ref
  6.6 0.0 copy-done
  6.7 52.3 %shard_map.85 = (f32[128,128]{1,0:T(8,128)S(1)}, f32[32,4096]{1,0:T(8,128)S(1)}, f32[128,128]{1,0:T(8,128)S(1)}) custom-call(bf16[8,32,64]{2,1,0:T(8,128)(2,1)S(1)} %bitcast.24, bf16[32,4096]{1,0:T(8,128)(2,1)S(1)} %stack.114.act_ref, bf16[4096,128]{1,0:T(8,128)(2,1)S(1)} %copy-done), custom_call_target="tpu_custom_call" | custom-call | tf_op jit(solution)/shard_map/pallas_call | solution.py:300
  58.9 0.7 %copy.25 = f32[64,2,128]{2,1,0:T(2,128)} copy(f32[64,2,128]{2,0,1:T(8,128)S(1)} %bitcast.25) | data formatting | bytes 131072 | tf_op jit(solution)/shard_map/transpose | solution.py:327
  59.6 0.8 %copy.30 = f32[32,4096]{1,0:T(8,128)} copy(f32[32,4096]{1,0:T(8,128)S(1)} %get-tuple-element.50) | data formatting | bytes 1048576
  60.4 0.6 %copy.31 = f32[128,128]{1,0:T(8,128)} copy(f32[128,128]{1,0:T(8,128)S(1)} %get-tuple-element.51) | data formatting | bytes 131072
  (12 shorter events, 0.1 us)
Async XLA Ops:
  0.6 6.0 %copy-start = (bf16[4096,128]{1,0:T(8,128)(2,1)S(1)}, bf16[4096,128]{1,0:T(8,128)(2,1)}, u32[]{:S(2)}) copy-start(bf16[4096,128]{1,0:T(8,128)(2,1)} %omega_ref.1) | copy-start | bytes 3145732

commit v2 on v1

--- a/solution.py
+++ b/solution.py
@@ -13,7 +13,7 @@
 RANK = 128
 ACT = 32768
 PANEL = 8
-COLS = 1024
+COLS = 2048
 
 INFL_RATE = 4.5
 DEFOCUS_RATE = 6.0
@@ -24,42 +24,39 @@
 COS_POLY = (1.4142135, -6.97885099, 5.73946117, -1.88356299, 0.310698192)
 
 
-def split3(value):
-    high = lax.reduce_precision(value, 8, 7)
-    middle = lax.reduce_precision(value - high, 8, 7)
-    low = lax.reduce_precision(value - high - middle, 8, 7)
-    return [high, middle, low]
+def split(value, parts):
+    pieces = []
+    for _ in range(parts):
+        piece = value.astype(jnp.bfloat16).astype(jnp.float32)
+        pieces.append(piece)
+        value = value - piece
+    return pieces
 
 
 def pixel_features(pixels, wave_scale, flux_level):
     u = (pixels // FOCAL - FOCAL // 2).astype(jnp.float32)
     v = (pixels % FOCAL - FOCAL // 2).astype(jnp.float32)
     radius = u * u + v * v
-    amplitude = flux_level * jnp.exp(-INFL_RATE * radius / (FOCAL * FOCAL))
+    amplitude = flux_level * jnp.exp(-INFL_RATE / (FOCAL * FOCAL) * radius)
     step_u = -(wave_scale / FOCAL) * u
     step_v = -(wave_scale / FOCAL) * v
     defocus = radius * (DEFOCUS_RATE / (FOCAL * FOCAL)) / wave_scale
     rows = []
-    for turns in (step_u, step_v, defocus):
-        rows += split3(turns - jnp.round(turns))
+    for turns, parts in ((step_u, 3), (step_v, 3), (defocus, 2)):
+        rows += split(turns - jnp.round(turns), parts)
     one, zero = jnp.ones_like(u), jnp.zeros_like(u)
-    rows += [one] * 3 + [zero] * 4
-    high, middle, low = split3(amplitude)
-    rows += [high, high, high, middle, middle, low] + [zero] * 10
-    return jnp.stack(rows)
-
-
-def actuator_features(codes, field):
+    high, low = split(amplitude, 2)
+    return rows + [one, one, high, high, low, low, zero, zero]
+
+
+def actuator_features(codes, field_re, field_im):
     mirror = (codes // (GRID * GRID)).astype(jnp.float32)
     x = (codes // GRID % GRID - GRID // 2).astype(jnp.float32)
     y = (codes % GRID - GRID // 2).astype(jnp.float32)
     zero = jnp.zeros_like(x)
-    angle = jnp.arctan2(field[1], field[0]) * (0.5 / math.pi)
-    magnitude = jnp.sqrt(field[0] * field[0] + field[1] * field[1])
-    rows = [x] * 3 + [y] * 3 + [mirror] * 3 + split3(angle) + [zero] * 4
-    high, middle, low = split3(magnitude)
-    rows += [high, middle, low, high, middle, high] + [zero] * 10
-    return jnp.stack(rows).astype(jnp.bfloat16)
+    angle = jnp.arctan2(field_im, field_re) * (0.5 / math.pi)
+    high, low = split(jnp.sqrt(field_re * field_re + field_im * field_im), 2)
+    return [x] * 3 + [y] * 3 + [mirror] * 2 + split(angle, 2) + [high, low, high, low, zero, zero]
 
 
 def dot_first(lhs, rhs, precision=None):
@@ -69,8 +66,10 @@
 
 
 def jacobian_tile(pix, act):
-    turns = dot_first(pix[:16], act[:16])
-    scale = dot_first(pix[16:], act[16:])
+    row = lax.broadcasted_iota(jnp.int32, pix.shape, 0)
+    none = jnp.zeros_like(pix)
+    turns = dot_first(jnp.where(row < 10, pix, none), act)
+    scale = dot_first(jnp.where(row < 10, none, pix), act)
     f = turns - jnp.round(turns)
     q = f * f
     sine = SIN_POLY[-1]
@@ -86,9 +85,9 @@
 
 
 def kernel(
-    A, Z, pix_ref, act_ref, omega_ref, basis_ref, proj_ref, rfac_ref,
-    pix_all, act_all, rs_send, rs_recv, own, sk_all, jac, aug, tmat, ex_send, ex_recv,
-    feat_s, feat_r, rs_s, rs_r, z_s, z_r, pl_s, pl_r, ex_s, ex_r, local_s,
+    A, Z, index_ref, codes_ref, field_ref, scale_ref, flux_ref, omega_ref, basis_ref, proj_ref, rfac_ref,
+    rows_ref, pix_ref, act_ref, pix_all, act_all, rs_send, rs_recv, own, sk_all, jac, aug, tmat, ex_send, ex_recv,
+    feat_s, feat_r, rs_s, rs_r, z_s, z_r, pl_s, pl_r, sib_s, ex_s, ex_r,
 ):
     ai, zi = lax.axis_index("act"), lax.axis_index("pix")
     rows_blk = rs_send.shape[1]
@@ -111,6 +110,16 @@
 
     for k in range(1, Z):
         pl.semaphore_signal(barrier, inc=1, device_id=(ai, pix_peer(k)), device_id_type=MESH)
+
+    block = pix_ref.shape[2]
+    for at, row in enumerate(pixel_features(index_ref[...], scale_ref[0], flux_ref[0])):
+        rows_ref[at:at + 1, :A * block] = row
+    for a in range(A):
+        pix_ref[a] = rows_ref[:, a * block:(a + 1) * block].astype(jnp.bfloat16)
+    features = actuator_features(codes_ref[...], field_ref[0, 0:1], field_ref[0, 1:2])
+    for at, row in enumerate(features):
+        rows_ref[at:at + 1, :cols] = row
+    act_ref[...] = rows_ref[:, :cols].astype(jnp.bfloat16)
     pl.semaphore_wait(barrier, A - 1 + Z - 1)
 
     def feat_copies(peer, slot):
@@ -177,33 +186,56 @@
     for k in range(1, Z):
         z_copy(pix_peer(k), zi).start()
 
+    sibling = ai + 1 - 2 * lax.rem(ai, 2)
+
     def spread(channel):
-        @pl.loop(1, A)
-        def _(k):
-            plane_copy(channel, act_peer(k), ai).start()
+        @pl.loop(1, A // 2)
+        def _(k):
+            plane_copy(channel, act_peer(2 * k), ai).start()
+
+        pass_on(channel, ai).start()
+
+    def pass_on(channel, shard):
+        return pltpu.make_async_remote_copy(
+            src_ref=sk_all.at[block_of(channel, shard)], dst_ref=sk_all.at[block_of(channel, shard)],
+            send_sem=sib_s.at[channel, shard], recv_sem=pl_r.at[channel, shard],
+            device_id=(sibling, zi), device_id_type=MESH)
+
+    def forward(channel):
+        @pl.loop(1, A // 2)
+        def _(k):
+            shard = act_peer(2 * k)
+            plane_copy(channel, shard, shard).wait_recv()
+            pass_on(channel, shard).start()
 
     def fill(channel):
         @pl.loop(0, A)
         def _(a):
             jac[block_of(channel, a)] = jacobian_tile(pix_all[channel, a], act_all[channel])
 
+    early = Z // 2
     spread(zi)
     fill(zi)
     for k in range(1, Z):
         z_copy(pix_peer(k), pix_peer(k)).wait_recv()
         spread(pix_peer(k))
+    forward(zi)
     for k in range(1, Z):
         for copy in feat_copies(pix_peer(k), pix_peer(k)):
             copy.wait_recv()
+    for k in range(1, early):
+        fill(pix_peer(k))
+
     @pl.loop(1, Z)
     def _(k):
-        fill(pix_peer(k))
+        forward(pix_peer(k))
 
     @pl.loop(0, Z)
     def _(c):
-        @pl.loop(1, A)
-        def _(k):
-            plane_copy(c, act_peer(k), act_peer(k)).wait_recv()
+        @pl.loop(0, A // 2)
+        def _(k):
+            shard = lax.rem(sibling + 2 * k, A)
+            pass_on(c, shard).wait_recv()
 
     sketch = sk_all[...]
     aug[:, :RANK] = dot_first(sketch, sketch)
@@ -212,7 +244,7 @@
     aug[:, RANK:] = (row_id == col_id).astype(jnp.float32)
     tmat[...] = jnp.zeros_like(tmat)
     panels = RANK // PANEL
-    span = sk_all.shape[0] // panels
+    late = (Z - early) * A // panels
     sub = lax.broadcasted_iota(jnp.int32, (PANEL, RANK), 0)
     lane = lax.broadcasted_iota(jnp.int32, (PANEL, RANK), 1)
 
@@ -236,8 +268,13 @@
         factor = jnp.where(lane >= at + PANEL, left, 0.0)
         both = jnp.concatenate([left, right], axis=1)
         aug[...] = aug[...] - dot_first(factor, both, HIGH)
-        rows = pl.ds(pl.multiple_of(i * span, span), span)
-        tmat[...] += dot_first(sk_all[rows], jac[rows])
+        for n in range(late):
+            at = i * late + n
+            done = block_of(pix_peer(at // A), lax.rem(at, A))
+            tmat[...] += dot_first(sk_all[done], jac[done])
+            channel, shard = pix_peer(early + at // A), lax.rem(at, A)
+            tile = jacobian_tile(pix_all[channel, shard], act_all[channel])
+            tmat[...] += dot_first(sk_all[block_of(channel, shard)], tile)
 
     inverse_l = aug[:, RANK:]
     rfac_ref[...] = jnp.where(col_id >= row_id, aug[:, :RANK], 0.0) * (
@@ -270,9 +307,13 @@
 
     @pl.loop(0, Z)
     def _(c):
-        @pl.loop(1, A)
-        def _(k):
-            plane_copy(c, act_peer(k), ai).wait_send()
+        @pl.loop(1, A // 2)
+        def _(k):
+            plane_copy(c, act_peer(2 * k), ai).wait_send()
+
+        @pl.loop(0, A // 2)
+        def _(k):
+            pass_on(c, act_peer(2 * k)).wait_send()
 
     for k in range(1, Z):
         peer = pix_peer(k)
@@ -285,16 +326,13 @@
 
 def on_device(pixel_index, act_map, omega, pupil_field, channel_scale, channel_flux):
     A, Z = lax.axis_size("act"), lax.axis_size("pix")
-    pixels = pixel_index[0]
-    count = pixels.shape[0]
+    count = pixel_index.shape[1]
     cols = act_map.shape[0]
     part = cols // Z
     block = count // A
     rows_blk = 2 * block
-    pix = pixel_features(pixels, channel_scale[0], channel_flux[0])
-    pix = pix.reshape(32, A, block).transpose(1, 0, 2).astype(jnp.bfloat16)
-    act = actuator_features(act_map, pupil_field[0])
     vmem = pl.BlockSpec(memory_space=pltpu.VMEM)
+    smem = pl.BlockSpec(memory_space=pltpu.SMEM)
     dma = pltpu.SemaphoreType.DMA
     f32, bf16 = jnp.float32, jnp.bfloat16
     basis, projection, r_factor = pl.pallas_call(
@@ -304,11 +342,14 @@
             jax.ShapeDtypeStruct((RANK // Z, cols), f32),
             jax.ShapeDtypeStruct((RANK, RANK), f32),
         ),
-        in_specs=[vmem] * 3,
+        in_specs=[vmem] * 3 + [smem] * 2 + [vmem],
         out_specs=(vmem,) * 3,
         scratch_shapes=[
-            pltpu.VMEM((Z, A, 32, block), bf16),
-            pltpu.VMEM((Z, 32, part), bf16),
+            pltpu.VMEM((16, max(cols, count)), f32),
+            pltpu.VMEM((A, 16, block), bf16),
+            pltpu.VMEM((16, cols), bf16),
+            pltpu.VMEM((Z, A, 16, block), bf16),
+            pltpu.VMEM((Z, 16, part), bf16),
             pltpu.VMEM((A, rows_blk, RANK), f32),
             pltpu.VMEM((A, rows_blk, RANK), f32),
             pltpu.VMEM((rows_blk, RANK), f32),
@@ -319,11 +360,11 @@
             pltpu.VMEM((Z, RANK // Z, part), bf16),
             pltpu.VMEM((Z, RANK // Z, part), bf16),
             dma((Z, 2)), dma((Z, 2)), dma((A,)), dma((A,)), dma((Z,)), dma((Z,)),
-            dma((Z, A)), dma((Z, A)), dma((Z,)), dma((Z,)), dma,
+            dma((Z, A)), dma((Z, A)), dma((Z, A)), dma((Z,)), dma((Z,)),
         ],
         compiler_params=pltpu.CompilerParams(
             collective_id=0, has_side_effects=True, vmem_limit_bytes=48 * 1024 * 1024),
-    )(pix, act, omega)
+    )(pixel_index, act_map.reshape(1, cols), pupil_field, channel_scale, channel_flux, omega)
     basis_out = basis.reshape(2, block, RANK).transpose(1, 0, 2).reshape(1, rows_blk, RANK)
     return basis_out, projection, r_factor
 

time: 61.3 us -> 61.1 us (level)
  other arithmetic: 2.76 us -> 0 us
  Pallas kernels: 52.3 us -> 53.6 us
  local copies, waits for them, and re-layouts: 3.87 us -> 4.81 us
    unnamed x4 -> x10, local copies, waits for them, and re-layouts: 1.43 us -> 4.13 us
    another operation x5 -> x0, other arithmetic: 2.05 us -> none
    another operation x25 -> x0, local copies, waits for them, and re-layouts: 1.76 us -> none  [the longest x16 1.05 us: pixel_features(): return jnp.stack(rows)]
    pallas_call x1, Pallas kernels: 52.3 us -> 53.6 us  [on_device(): pl.pallas_call(functools.partial(kernel, A, Z), out_shape=(jax.ShapeDtype...]
    mul x1 -> x0, other arithmetic: 0.71 us -> none  [pixel_features(): amplitude = flux_level * jnp.exp(-INFL_RATE * radius / (FOCAL * FOCAL))]
where the time goes in v2:
time: 61.1 us; the launch traced here: 60.3 us
  Pallas kernels  53.6 us (88%)
  local copies, waits for them, and re-layouts  4.81 us (8%)
  between operations  1.96 us (3%)
    pallas_call x1, Pallas kernels, on_device(): pl.pallas_call(functools.partial(kernel, A, Z), out_shape=(jax.ShapeDtype...  53.6 us
    unnamed x10, local copies, waits for them, and re-layouts  4.13 us

profile of v2, /device:TPU:0, one launch (start us, length us, event | category | flops | bytes accessed | tf_op | source)
XLA Modules:
  0.0 60.3 jit_solution(12565724151477750689)
XLA Ops:
  1.3 0.0 copy-start.3
  1.9 0.0 copy-done.3
  2.0 0.0 copy-start
  2.0 1.2 %copy-done = bf16[4096,128]{1,0:T(8,128)(2,1)S(1)} copy-done((bf16[4096,128]{1,0:T(8,128)(2,1)S(1)}, bf16[4096,128]{1,0:T(8,128)(2,1)}, u32[]{:S(2)}) %copy-start) | copy-done | bytes 1048600
  3.2 0.0 copy-start.1
  3.2 0.8 %copy-done.1 = f32[1,2,4096]{2,1,0:T(2,128)S(1)} copy-done((f32[1,2,4096]{2,1,0:T(2,128)S(1)}, f32[1,2,4096]{2,1,0:T(2,128)}, u32[]{:S(2)}) %copy-start.1) | copy-done | bytes 32792
  3.9 0.0 copy-start.2
  3.9 0.7 %copy-done.2 = s32[4096]{0:T(1024)S(1)} copy-done((s32[4096]{0:T(1024)S(1)}, s32[4096]{0:T(1024)}, u32[]{:S(2)}) %copy-start.2) | copy-done | bytes 16408
  4.7 53.6 %shard_map.85 = (f32[128,128]{1,0:T(8,128)S(1)}, f32[32,4096]{1,0:T(8,128)S(1)}, f32[128,128]{1,0:T(8,128)S(1)}) custom-call(s32[1,512]{1,0:T(1,128)S(1)} %copy-done.3, s32[1,4096]{1,0:T(1,128)S(1)} %bitcast.6, f32[1,2,4096]{2,1,0:T(2,128)S(1)} %copy-done.1, f32[1]{0:T(128)S(6)} %copy.12.scale_ref, f32[1]{0:T(128)S(6)} %copy.13.flux_ref, ...), custom_call_target="tpu_custom_call" | custom-call | tf_op jit(solution)/shard_map/pallas_call | solution.py:338
  58.2 0.7 %copy.9 = f32[64,2,128]{2,1,0:T(2,128)} copy(f32[64,2,128]{2,0,1:T(8,128)S(1)} %bitcast.5) | data formatting | bytes 131072 | tf_op jit(solution)/shard_map/transpose | solution.py:368
  58.9 0.8 %copy.14 = f32[32,4096]{1,0:T(8,128)} copy(f32[32,4096]{1,0:T(8,128)S(1)} %get-tuple-element.13) | data formatting | bytes 1048576
  59.7 0.6 %copy.15 = f32[128,128]{1,0:T(8,128)} copy(f32[128,128]{1,0:T(8,128)S(1)} %get-tuple-element.14) | data formatting | bytes 131072
Async XLA Ops:
  1.3 0.7 %copy-start.3 = (s32[1,512]{1,0:T(1,128)S(1)}, s32[1,512]{1,0:T(1,128)}, u32[]{:S(2)}) copy-start(s32[1,512]{1,0:T(1,128)} %index_ref.1) | copy-start | bytes 6148
  2.0 1.2 %copy-start = (bf16[4096,128]{1,0:T(8,128)(2,1)S(1)}, bf16[4096,128]{1,0:T(8,128)(2,1)}, u32[]{:S(2)}) copy-start(bf16[4096,128]{1,0:T(8,128)(2,1)} %omega_ref.1) | copy-start | bytes 3145732
  3.2 0.8 %copy-start.1 = (f32[1,2,4096]{2,1,0:T(2,128)S(1)}, f32[1,2,4096]{2,1,0:T(2,128)}, u32[]{:S(2)}) copy-start(f32[1,2,4096]{2,1,0:T(2,128)} %field_ref.1) | copy-start | bytes 98308
  3.9 0.7 %copy-start.2 = (s32[4096]{0:T(1024)S(1)}, s32[4096]{0:T(1024)}, u32[]{:S(2)}) copy-start(s32[4096]{0:T(1024)} %param.7) | copy-start | bytes 49156
